TPU v7x, 256 devices: a whole 4x4x8 slice. The times are simulated.
256 devices in a mesh: stn: 32 (over z, x_hi, core), chan: 8 (over y, x_lo).
Axes of the slice: x: 4 (x_hi: 2, x_lo: 2; x = x_hi * 2 + x_lo), y: 4, z: 8, core: 2. Of those that a mesh axis runs over, the one named last changes fastest.
Arguments:
- screen: float32 [64, 512, 512], P('stn'), may hold values from -6 to 6
- pierce_coords: float32 [2, 32, 8, 32, 128], P(None, 'stn', 'chan'), may hold values from 0 to 1
- query_dest: int32 [32, 8, 32, 128], P('stn', 'chan'), may hold values from 0 to 1024, as said below
- positions: float32 [3, 512], P(None, 'stn'), may hold values from -50 to 50
- directions: float32 [3, 512], replicated, may hold values from -0.7 to 0.7
- freq_ratio: float32 [256], P('chan'), may hold values from 0.7 to 1.4
- source_flux: float32 [512], replicated, may hold values from 0.2 to 5
- spectral_index: float32 [512], replicated, may hold values from -1.5 to 0.5
Outputs:
- visibilities: float32 [256, 2, 512, 512], P('chan', None, 'stn')
Inputs may be any that keep to these rules, and one draw needn't show every extreme that they name: `query_dest`: in each block every number 0 to 1023 appears in exactly one slot and empty slots hold 1024; an owner's live slots come first in its row; one owner, the same for every block, has all 128 of its slots live in every block.
All inputs are finite; a program needn't handle non-finite values.
Results may differ from a plain program's by a relative error of at most 0.008.
Values may be sent and summed in bfloat16 or wider, within the bound.
A program may use at most 128 MiB of HBM per device.

v0:
```python
import math
import jax
import jax.numpy as jnp
from jax import lax
from jax.sharding import PartitionSpec as P

TWO_PI = 2.0 * math.pi


def interpolate(values, coords, strip_rows, tile_cols):
    row_pos = coords[0] * (strip_rows - 1)
    col_pos = coords[1] * (tile_cols - 1)
    row_low = jnp.clip(jnp.floor(row_pos), 0.0, strip_rows - 2.0)
    col_low = jnp.clip(jnp.floor(col_pos), 0.0, tile_cols - 2.0)
    frac_y = row_pos - row_low
    frac_x = col_pos - col_low
    corner = row_low.astype(jnp.int32) * tile_cols + col_low.astype(jnp.int32)
    lower_pair = (1.0 - frac_x) * values[corner] + frac_x * values[corner + 1]
    upper_pair = (1.0 - frac_x) * values[corner + tile_cols] + frac_x * values[
        corner + tile_cols + 1
    ]
    return (1.0 - frac_y) * lower_pair + frac_y * upper_pair


def make_phasors(station_rows, iono_rows, directions, freq_ratio):
    delays = (
        station_rows[:, 0:1] * directions[0][None, :]
        + station_rows[:, 1:2] * directions[1][None, :]
    )
    delays = delays + station_rows[:, 2:3] * directions[2][None, :]
    angles = (TWO_PI * freq_ratio)[None, :, None] * delays[:, None, :] + iono_rows[
        :, None, :
    ] / freq_ratio[None, :, None]
    return jnp.concatenate([jnp.cos(angles), jnp.sin(angles)], axis=-1).astype(jnp.bfloat16)


def spectrum(source_flux, spectral_index, freq_ratio, count):
    return (
        source_flux[None, :]
        * jnp.exp(spectral_index[None, :] * jnp.log(freq_ratio)[:, None])
        / math.sqrt(count)
    )


def weight_rows(phasors, intensity):
    sources = intensity.shape[1]
    real_part = (phasors[:, :, :sources].astype(jnp.float32) * intensity[None]).astype(jnp.bfloat16)
    imag_part = (phasors[:, :, sources:].astype(jnp.float32) * intensity[None]).astype(jnp.bfloat16)
    upper_rows = jnp.concatenate([real_part, imag_part], axis=-1)
    lower_rows = jnp.concatenate([imag_part, -real_part], axis=-1)
    return jnp.concatenate([upper_rows, lower_rows], axis=0)


def body(
    screen,
    pierce_coords,
    query_dest,
    positions,
    directions,
    freq_ratio,
    source_flux,
    spectral_index,
):
    groups = lax.axis_size("stn")
    tile_cols = screen.shape[2]
    strip_rows = screen.shape[0] * screen.shape[1]
    values = screen.reshape(-1)
    capacity = query_dest.shape[3]
    coords = pierce_coords.reshape(2, groups, capacity)
    sampled = interpolate(
        values,
        lax.all_to_all(coords, "stn", split_axis=1, concat_axis=1, tiled=True),
        strip_rows,
        tile_cols,
    )
    returned = lax.all_to_all(sampled, "stn", split_axis=0, concat_axis=0, tiled=True)
    stations_local = positions.shape[1]
    local_sources = source_flux.shape[0] // lax.axis_size("chan")
    queries = stations_local * local_sources
    buffer = (
        jnp.zeros((queries + 1,), jnp.float32).at[query_dest.reshape(-1)].set(returned.reshape(-1))
    )
    own_iono = buffer[:queries].reshape(stations_local, local_sources)
    iono_phase = lax.all_gather(own_iono, "chan", axis=1, tiled=True)
    station_rows = positions.T
    own_phasors = make_phasors(station_rows, iono_phase, directions, freq_ratio)
    intensity = spectrum(source_flux, spectral_index, freq_ratio, source_flux.shape[0])
    weighted = weight_rows(own_phasors, intensity)
    total_stations = stations_local * groups
    channels = freq_ratio.shape[0]
    columns = jnp.einsum(
        "ack,nck->can",
        weighted,
        lax.all_gather(own_phasors, "stn", axis=0, tiled=True),
        preferred_element_type=jnp.float32,
    )
    visible = columns.reshape(channels, 2, stations_local, total_stations)
    first_row = lax.axis_index("stn") * stations_local
    rows_global = first_row + jnp.arange(stations_local, dtype=jnp.int32)
    cross_only = rows_global[:, None] != jnp.arange(total_stations, dtype=jnp.int32)[None, :]
    return jnp.where(cross_only[None, None], visible, jnp.zeros_like(visible))


def solution(mesh):
    in_specs = (
        P("stn", None, None),
        P(None, "stn", "chan", None, None),
        P("stn", "chan", None, None),
        P(None, "stn"),
        P(),
        P("chan"),
        P(),
        P(),
    )
    out_specs = P("chan", None, "stn", None)
    return jax.shard_map(body, mesh=mesh, in_specs=in_specs, out_specs=out_specs, check_vma=False)
```

profile of v0, /device:TPU:1, one launch (start us, length us, event | category | flops | bytes accessed | tf_op | source)
XLA Modules:
  0.0 433.8 jit_solution(1635080177208044203)
XLA Ops:
  6.5 1.4 copy.16
  7.9 12.6 %all-to-all-start = ((f32[2,32,128]{2,0,1:T(2,128)}), f32[2,32,128]{2,0,1:T(2,128)S(1)}, u32[]{:S(2)}, u32[]{:S(2)}) async-start(f32[2,32,128]{2,0,1:T(2,128)} %bitcast.85), calls=%async_computation | async-start | bytes 65536 | tf_op jit(solution)/shard_map/all_to_all | solution.py:72
  20.5 0.7 compare_select_fusion
  21.3 0.8 fusion.27
  22.1 0.7 fusion.28
  22.7 0.8 multiply_multiply_fusion
  23.5 0.8 slice_bitcast_fusion.2
  24.3 2.1 copy.14
  26.5 3.7 all-to-all-done
  30.1 0.1 multiply_add_fusion.1
  30.2 23.0 %gather_fusion = f32[4096]{0:T(1024)S(1)} fusion(f32[524288]{0:T(1024)S(1)} %bitcast.88, s32[4096]{0:T(1024)S(1)} %get-tuple-element.11), kind=kCustom, calls=%fused_computation | custom fusion | bytes 49152 | tf_op jit(solution)/shard_map/gather | solution.py:18
  53.3 23.0 %gather_fusion.1 = f32[4096]{0:T(1024)S(1)} fusion(f32[524288]{0:T(1024)S(1)} %bitcast.89, s32[4096]{0:T(1024)S(1)} %get-tuple-element.12), kind=kCustom, calls=%fused_computation.1 | custom fusion | bytes 49152 | tf_op jit(solution)/shard_map/gather | solution.py:18
  76.3 23.0 %gather_fusion.2 = f32[4096]{0:T(1024)S(1)} fusion(f32[524288]{0:T(1024)S(1)} %bitcast.90, s32[4096]{0:T(1024)S(1)} %get-tuple-element.13), kind=kCustom, calls=%fused_computation.2 | custom fusion | bytes 49152 | tf_op jit(solution)/shard_map/gather | solution.py:19
  99.4 0.0 copy-start
  99.4 23.0 %gather_fusion.3 = f32[4096]{0:T(1024)S(1)} fusion(f32[524288]{0:T(1024)S(1)} %bitcast.91, s32[4096]{0:T(1024)S(1)} %get-tuple-element.14), kind=kCustom, calls=%fused_computation.3 | custom fusion | bytes 49152 | tf_op jit(solution)/shard_map/gather | solution.py:19
  122.5 0.6 fusion.18
  123.1 6.1 %all-to-all-start.1 = ((f32[32,1,128]{2,1,0:T(1,128)}), f32[32,1,128]{2,1,0:T(1,128)S(1)}, u32[]{:S(2)}, u32[]{:S(2)}) async-start(f32[32,1,128]{2,1,0:T(1,128)} %bitcast.21), calls=%async_computation.1 | async-start | bytes 32768 | tf_op jit(solution)/shard_map/all_to_all | solution.py:76
  129.2 0.0 all-gather.3.cloned.1.call-start
  129.2 0.1 multiply_add_fusion
  129.3 9.2 %all-to-all-done.1 = f32[32,1,128]{2,1,0:T(1,128)S(1)} async-done(((f32[32,1,128]{2,1,0:T(1,128)}), f32[32,1,128]{2,1,0:T(1,128)S(1)}, u32[]{:S(2)}, u32[]{:S(2)}) %all-to-all-start.1) | async-done | bytes 16416 | tf_op jit(solution)/shard_map/all_to_all | solution.py:76
  138.5 15.5 %scatter_custom_fusion = f32[1025]{0:T(1024)S(1)} fusion(s32[4096]{0:T(1024)S(1)} %bitcast.101, f32[4096]{0:T(1024)S(1)} %bitcast.102, f32[]{:T(128)} %constant.11.clone.1), kind=kCustom, calls=%fused_computation.55 | custom fusion | bytes 4104 | tf_op jit(solution)/shard_map/scatter | solution.py:81
  154.0 0.1 reshape.419
  154.1 22.4 %all-gather = f32[8,64,16]{1,2,0:T(8,128)S(1)} all-gather(f32[1,64,16]{1,2,0:T(8,128)S(1)} %bitcast.99), channel_id=1, replica_groups=mesh['stn'=32,'chan'=8] {'chan'}, dimensions={0}, use_global_device_ids=true | all-gather | bytes 36864 | tf_op jit(solution)/shard_map/all_gather | solution.py:84
  176.5 0.1 reshape.473
  176.6 0.0 copy-done
  176.6 4.3 multiply_convert_fusion.1
  180.9 1.1 pad_maximum_fusion
  182.0 0.0 all-gather.3.cloned.1.call-update
  182.0 0.1 iota_compare_fusion
  182.1 3.9 fusion.26
  186.0 223.9 %all-gather.3.cloned.1.call-done = bf16[512,32,1024]{2,0,1:T(8,128)(2,1)} async-done(((bf16[16,32,1024]{2,0,1:T(8,128)(2,1)}), bf16[512,32,1024]{2,0,1:T(8,128)(2,1)}) %all-gather.3.cloned.1.call-update) | async-done | bytes 33554448 | tf_op jit(solution)/shard_map/all_gather | solution.py:94
  410.0 15.4 %fusion = f32[32,32,512]{2,1,0:T(8,128)S(1)} fusion(bf16[512,32,1024]{2,0,1:T(8,128)(2,1)} %all-gather.3.cloned.1.call-done, bf16[16,32,512]{2,0,1:T(8,128)(2,1)S(1)} %fusion.26, bf16[16,32,512]{2,0,1:T(8,128)(2,1)S(1)} %get-tuple-element.6, bf16[16,32,512]{2,0,1:T(8,128)(2,1)S(1)} %get-tuple-element.5), kind=kOutput, calls=%fused_computation.5 | convolution fusion | flops 1082130432 | bytes 37224448 | tf_op jit(solution)/shard_map/ack,nck->can/dot_general | solution.py:91
  425.4 1.6 broadcast_select_fusion
  (5 shorter events, 0.1 us)
Async XLA Ops:
  7.9 22.2 %all-to-all-start = ((f32[2,32,128]{2,0,1:T(2,128)}), f32[2,32,128]{2,0,1:T(2,128)S(1)}, u32[]{:S(2)}, u32[]{:S(2)}) async-start(f32[2,32,128]{2,0,1:T(2,128)} %bitcast.85), calls=%async_computation | async-start | bytes 65536 | tf_op jit(solution)/shard_map/all_to_all | solution.py:72
  99.4 77.2 %copy-start = (f32[32]{0:T(128)S(1)}, f32[32]{0:T(128)}, u32[]{:S(2)}) copy-start(f32[32]{0:T(128)} %param.13) | copy-start | bytes 388
  123.1 15.4 %all-to-all-start.1 = ((f32[32,1,128]{2,1,0:T(1,128)}), f32[32,1,128]{2,1,0:T(1,128)S(1)}, u32[]{:S(2)}, u32[]{:S(2)}) async-start(f32[32,1,128]{2,1,0:T(1,128)} %bitcast.21), calls=%async_computation.1 | async-start | bytes 32768 | tf_op jit(solution)/shard_map/all_to_all | solution.py:76
  129.2 280.8 %all-gather.3.cloned.1.call-start = ((), (), s32[]{:S(2)}) async-start(), calls=%async_computation.2 | async-start | bytes 34603008 | tf_op jit(solution)/shard_map/all_gather | solution.py:94
Sparse Core Ops, SparseCore 0:
  182.1 227.7 all-gather.2
where the time goes:
time: 434 us
  waiting for transfers between devices  237 us (55%)
  local copies, waits for them, and re-layouts  113 us (26%)
  blocking collectives  22.4 us (5%)
  starting transfers between devices  18.7 us (4%)
  matrix products  15.4 us (4%)
  other arithmetic  14 us (3%)
  between operations  13.5 us (3%)
    all_gather x1, waiting for transfers between devices, body(): lax.all_gather(own_phasors, 'stn', axis=0, tiled=True)  224 us
    gather x2, local copies, waits for them, and re-layouts, interpolate(): lower_pair = (1.0 - frac_x) * values[corner] + frac_x * values[corner + 1]  46.1 us
    gather x1, local copies, waits for them, and re-layouts, interpolate(): values[corner + tile_cols]  23 us
    gather x1, local copies, waits for them, and re-layouts, interpolate(): values[corner + tile_cols + 1]  23 us
    all_gather x1, blocking collectives, body(): iono_phase = lax.all_gather(own_iono, 'chan', axis=1, tiled=True)  22.4 us
    scatter x1, local copies, waits for them, and re-layouts, body(): jnp.zeros((queries + 1,), jnp.float32).at[query_dest.reshape(-1)]  15.5 us
    dot_general x1, matrix products, body(): jnp.einsum('ack,nck->can', weighted, lax.all_gather(own_phasors, 'stn', a...  15.4 us
    all_to_all x1, starting transfers between devices, body(): lax.all_to_all(coords, 'stn', split_axis=1, concat_axis=1, tiled=True)  12.6 us
  transfers between devices with their start and end apart: 3, of which 3 were waited for; matrix products, arithmetic and copies ran while one was open for 2% of the time, Pallas kernels for 0%

commit v1 on v0

--- a/solution.py
+++ b/solution.py
@@ -91,7 +91,9 @@
     columns = jnp.einsum(
         "ack,nck->can",
         weighted,
-        lax.all_gather(own_phasors, "stn", axis=0, tiled=True),
+        jnp.concatenate(
+            lax.all_to_all(jnp.stack([own_phasors] * lax.axis_size("stn")), "stn", 0, 0), axis=0
+        ),
         preferred_element_type=jnp.float32,
     )
     visible = columns.reshape(channels, 2, stations_local, total_stations)

time: 434 us -> 965 us (2.22)
  waiting for transfers between devices: 237 us -> 736 us
  local copies, waits for them, and re-layouts: 113 us -> 147 us
  between operations: 13.5 us -> 0.16 us
  starting transfers between devices: 18.7 us -> 30.6 us
    all_to_all x0 -> x1, waiting for transfers between devices: none -> 723 us  [body(): lax.all_to_all(jnp.stack([own_phasors] * lax.axis_size('stn')), 'stn', 0, 0)]
    all_gather x1 -> x0, waiting for transfers between devices: 224 us -> none  [body(): lax.all_gather(own_phasors, 'stn', axis=0, tiled=True)]
    all_to_all x0 -> x1, local copies, waits for them, and re-layouts: none -> 22.9 us  [body(): lax.all_to_all(jnp.stack([own_phasors] * lax.axis_size('stn')), 'stn', 0, 0)]
    all_to_all x0 -> x1, starting transfers between devices: none -> 11.9 us  [body(): lax.all_to_all(jnp.stack([own_phasors] * lax.axis_size('stn')), 'stn', 0, 0)]
    another operation x0 -> x1, local copies, waits for them, and re-layouts: none -> 11 us  [body(): jnp.stack([own_phasors] * lax.axis_size('stn'))]
  transfers between devices with their start and end apart: 3 -> 3, of which waited for: 3 -> 3; matrix products, arithmetic and copies ran while one was open for 2% -> 1% of each run, Pallas kernels for 0% -> 0%
where the time goes in v1:
time: 965 us; the launch traced here: 964 us
  waiting for transfers between devices  736 us (76%)
  local copies, waits for them, and re-layouts  147 us (15%)
  starting transfers between devices  30.6 us (3%)
  blocking collectives  22.4 us (2%)
  matrix products  15.4 us (2%)
  other arithmetic  13 us (1%)
    all_to_all x1, waiting for transfers between devices, body(): lax.all_to_all(jnp.stack([own_phasors] * lax.axis_size('stn')), 'stn', 0, 0)  723 us
    gather x2, local copies, waits for them, and re-layouts, interpolate(): lower_pair = (1.0 - frac_x) * values[corner] + frac_x * values[corner + 1]  46.1 us
    gather x1, local copies, waits for them, and re-layouts, interpolate(): values[corner + tile_cols]  23 us
    gather x1, local copies, waits for them, and re-layouts, interpolate(): values[corner + tile_cols + 1]  23 us
    all_to_all x1, local copies, waits for them, and re-layouts, body(): lax.all_to_all(jnp.stack([own_phasors] * lax.axis_size('stn')), 'stn', 0, 0)  22.9 us
    all_gather x1, blocking collectives, body(): iono_phase = lax.all_gather(own_iono, 'chan', axis=1, tiled=True)  22.4 us
  transfers between devices with their start and end apart: 3, of which 3 were waited for; matrix products, arithmetic and copies ran while one was open for 1% of the time, Pallas kernels for 0%

profile of v1, /device:TPU:1, one launch (start us, length us, event | category | flops | bytes accessed | tf_op | source)
XLA Modules:
  0.0 964.0 jit_solution(2890009163461603549)
XLA Ops:
  0.0 1.4 copy.18
  1.4 12.6 %all-to-all-start = ((f32[2,32,128]{2,0,1:T(2,128)}), f32[2,32,128]{2,0,1:T(2,128)S(1)}, u32[]{:S(2)}, u32[]{:S(2)}) async-start(f32[2,32,128]{2,0,1:T(2,128)} %bitcast.86), calls=%async_computation | async-start | bytes 65536 | tf_op jit(solution)/shard_map/all_to_all | solution.py:72
  14.0 0.7 compare_select_fusion
  14.7 0.8 fusion.27
  15.5 0.7 fusion.28
  16.2 0.8 multiply_multiply_fusion
  17.0 0.8 slice_bitcast_fusion.2
  17.8 2.1 copy.16
  19.9 3.7 all-to-all-done
  23.6 0.1 multiply_add_fusion.1
  23.7 23.0 %gather_fusion = f32[4096]{0:T(1024)S(1)} fusion(f32[524288]{0:T(1024)S(1)} %bitcast.89, s32[4096]{0:T(1024)S(1)} %get-tuple-element.11), kind=kCustom, calls=%fused_computation | custom fusion | bytes 49152 | tf_op jit(solution)/shard_map/gather | solution.py:18
  46.8 23.0 %gather_fusion.1 = f32[4096]{0:T(1024)S(1)} fusion(f32[524288]{0:T(1024)S(1)} %bitcast.90, s32[4096]{0:T(1024)S(1)} %get-tuple-element.12), kind=kCustom, calls=%fused_computation.1 | custom fusion | bytes 49152 | tf_op jit(solution)/shard_map/gather | solution.py:18
  69.8 23.0 %gather_fusion.2 = f32[4096]{0:T(1024)S(1)} fusion(f32[524288]{0:T(1024)S(1)} %bitcast.91, s32[4096]{0:T(1024)S(1)} %get-tuple-element.13), kind=kCustom, calls=%fused_computation.2 | custom fusion | bytes 49152 | tf_op jit(solution)/shard_map/gather | solution.py:19
  92.8 0.0 copy-start
  92.8 23.0 %gather_fusion.3 = f32[4096]{0:T(1024)S(1)} fusion(f32[524288]{0:T(1024)S(1)} %bitcast.92, s32[4096]{0:T(1024)S(1)} %get-tuple-element.14), kind=kCustom, calls=%fused_computation.3 | custom fusion | bytes 49152 | tf_op jit(solution)/shard_map/gather | solution.py:19
  115.9 0.6 fusion.18
  116.6 6.1 all-to-all-start.1
  122.7 0.1 multiply_add_fusion
  122.7 9.2 all-to-all-done.1
  131.9 15.5 %scatter_custom_fusion = f32[1025]{0:T(1024)S(1)} fusion(s32[4096]{0:T(1024)S(1)} %bitcast.103, f32[4096]{0:T(1024)S(1)} %bitcast.104, f32[]{:T(128)} %constant.11.clone.1), kind=kCustom, calls=%fused_computation.55 | custom fusion | bytes 4104 | tf_op jit(solution)/shard_map/scatter | solution.py:81
  147.5 0.1 reshape.429
  147.5 22.4 %all-gather = f32[8,64,16]{1,2,0:T(8,128)S(1)} all-gather(f32[1,64,16]{1,2,0:T(8,128)S(1)} %bitcast.101), channel_id=1, replica_groups=mesh['stn'=32,'chan'=8] {'chan'}, dimensions={0}, use_global_device_ids=true | all-gather | bytes 36864 | tf_op jit(solution)/shard_map/all_gather | solution.py:84
  170.0 0.1 reshape.484
  170.1 0.0 copy-done
  170.1 4.3 multiply_convert_fusion.1
  174.4 0.1 pad_maximum_fusion
  174.5 11.0 %stack.2 = bf16[32,16,32,1024]{3,1,2,0:T(8,128)(2,1)} broadcast(bf16[16,32,1024]{2,0,1:T(8,128)(2,1)S(1)} %pad_maximum_fusion), dimensions={1,2,3} | broadcast | bytes 34603008 | tf_op jit(solution)/shard_map/stack | solution.py:95
  185.5 11.9 %all-to-all-start.2 = ((bf16[32,16,32,1024]{3,1,2,0:T(8,128)(2,1)}), bf16[32,16,32,1024]{3,1,2,0:T(8,128)(2,1)}, u32[]{:S(2)}, u32[]{:S(2)}) async-start(bf16[32,16,32,1024]{3,1,2,0:T(8,128)(2,1)} %stack.2), calls=%async_computation.2 | async-start | bytes 67108864 | tf_op jit(solution)/shard_map/all_to_all | solution.py:95
  197.5 0.1 iota_compare_fusion
  197.5 3.9 fusion.26
  201.4 722.7 %all-to-all-done.2 = bf16[32,16,32,1024]{3,1,2,0:T(8,128)(2,1)} async-done(((bf16[32,16,32,1024]{3,1,2,0:T(8,128)(2,1)}), bf16[32,16,32,1024]{3,1,2,0:T(8,128)(2,1)}, u32[]{:S(2)}, u32[]{:S(2)}) %all-to-all-start.2) | async-done | bytes 33554464 | tf_op jit(solution)/shard_map/all_to_all | solution.py:95
  924.2 22.9 %copy.15 = bf16[32,16,32,1024]{3,1,0,2:T(8,128)(2,1)} copy(bf16[32,16,32,1024]{3,1,2,0:T(8,128)(2,1)} %all-to-all-done.2) | data formatting | bytes 67108864 | tf_op jit(solution)/shard_map/all_to_all | solution.py:95
  947.0 15.4 %fusion = f32[32,32,512]{2,1,0:T(8,128)S(1)} fusion(bf16[512,32,1024]{2,0,1:T(8,128)(2,1)} %bitcast.93, bf16[16,32,512]{2,0,1:T(8,128)(2,1)S(1)} %fusion.26, bf16[16,32,512]{2,0,1:T(8,128)(2,1)S(1)} %get-tuple-element.6, bf16[16,32,512]{2,0,1:T(8,128)(2,1)S(1)} %get-tuple-element.5), kind=kOutput, calls=%fused_computation.5 | convolution fusion | flops 1082130432 | bytes 37224448 | tf_op jit(solution)/shard_map/ack,nck->can/dot_general | solution.py:91
  962.4 1.6 broadcast_select_fusion
  (5 shorter events, 0.1 us)
Async XLA Ops:
  1.4 22.2 %all-to-all-start = ((f32[2,32,128]{2,0,1:T(2,128)}), f32[2,32,128]{2,0,1:T(2,128)S(1)}, u32[]{:S(2)}, u32[]{:S(2)}) async-start(f32[2,32,128]{2,0,1:T(2,128)} %bitcast.86), calls=%async_computation | async-start | bytes 65536 | tf_op jit(solution)/shard_map/all_to_all | solution.py:72
  92.8 77.2 %copy-start = (f32[32]{0:T(128)S(1)}, f32[32]{0:T(128)}, u32[]{:S(2)}) copy-start(f32[32]{0:T(128)} %param.13) | copy-start | bytes 388
  116.6 15.4 %all-to-all-start.1 = ((f32[32,1,128]{2,1,0:T(1,128)}), f32[32,1,128]{2,1,0:T(1,128)S(1)}, u32[]{:S(2)}, u32[]{:S(2)}) async-start(f32[32,1,128]{2,1,0:T(1,128)} %bitcast.21), calls=%async_computation.1 | async-start | bytes 32768 | tf_op jit(solution)/shard_map/all_to_all | solution.py:76
  185.5 738.6 %all-to-all-start.2 = ((bf16[32,16,32,1024]{3,1,2,0:T(8,128)(2,1)}), bf16[32,16,32,1024]{3,1,2,0:T(8,128)(2,1)}, u32[]{:S(2)}, u32[]{:S(2)}) async-start(bf16[32,16,32,1024]{3,1,2,0:T(8,128)(2,1)} %stack.2), calls=%async_computation.2 | async-start | bytes 67108864 | tf_op jit(solution)/shard_map/all_to_all | solution.py:95
